TPU v7x, 128 devices: a whole 4x4x4 slice. The times are simulated.
128 devices in a mesh: node: 16 (over y, x), local: 8 (over z, core).
Axes of the slice: x: 4, y: 4, z: 4, core: 2. Of those that a mesh axis runs over, the one named last changes fastest.
Arguments:
- tokens: bfloat16 [16384, 2048], P(('node', 'local')), may hold values from -6 to 6
- cotangent: bfloat16 [16384, 2048], P(('node', 'local')), may hold values from -6 to 6
- gates: bfloat16 [16384, 2], P(('node', 'local')), may hold values from 0.099609375 to 1
- expert_ids: int32 [16384, 2], P(('node', 'local')), may hold values from 0 to 127, as said below
- slots: int32 [16384, 2], P(('node', 'local')), may hold values from 0 to 3, as said below
- w_gate: bfloat16 [128, 2048, 1024], P(('node', 'local')), may hold values from -0.125 to 0.125
- w_up: bfloat16 [128, 2048, 1024], P(('node', 'local')), may hold values from -0.125 to 0.125
- w_down: bfloat16 [128, 1024, 2048], P(('node', 'local')), may hold values from -0.1875 to 0.1875
Outputs:
- grad_in: bfloat16 [16384, 2048], P(('node', 'local'))
- grad_gates: bfloat16 [16384, 2], P(('node', 'local'))
- grad_w_gate: bfloat16 [128, 2048, 1024], P(('node', 'local'))
- grad_w_up: bfloat16 [128, 2048, 1024], P(('node', 'local'))
- grad_w_down: bfloat16 [128, 1024, 2048], P(('node', 'local'))
Inputs may be any that keep to these rules, and one draw needn't show every extreme that they name: `expert_ids`: each token names two different experts; among the 128 tokens of one device no expert is named more than 4 times, and one expert is named exactly 4 times by the tokens of every device; among the tokens of one device, the pairs naming the experts held by one node group number exactly 16. Within the tokens of one device, the pairs naming one expert take the slots 0 to their count minus 1, each once.
All inputs are finite; a program needn't handle non-finite values.
Results may differ from a plain program's by a relative error of at most 0.012.
Values may be sent and summed in bfloat16 or wider, within the bound.
A program may use at most 128 MiB of HBM per device.

v0:
```python
import jax
import jax.numpy as jnp
from jax import lax
from jax.sharding import PartitionSpec as P


def expert_backward(rows_x, rows_dy, rows_gate, gate_w, up_w, down_w):
    gate_pre = jnp.dot(rows_x, gate_w, preferred_element_type=jnp.float32)
    up_pre = jnp.dot(rows_x, up_w, preferred_element_type=jnp.float32)
    sigmoid_gate = jax.nn.sigmoid(gate_pre)
    act = gate_pre * sigmoid_gate
    hidden = (act * up_pre).astype(jnp.bfloat16)
    gate_value = rows_gate.astype(jnp.float32)
    scaled = (gate_value[:, None] * rows_dy.astype(jnp.float32)).astype(jnp.bfloat16)
    d_hidden = jnp.dot(scaled, down_w.T, preferred_element_type=jnp.float32)
    expert_out = jnp.dot(hidden, down_w, preferred_element_type=jnp.float32)
    gate_term = jnp.sum(rows_dy.astype(jnp.float32) * expert_out, axis=-1).astype(jnp.bfloat16)
    d_gate_pre = (
        d_hidden * up_pre * sigmoid_gate * (1.0 + gate_pre * (1.0 - sigmoid_gate))
    ).astype(jnp.bfloat16)
    d_up_pre = (d_hidden * act).astype(jnp.bfloat16)
    row_grad = (
        jnp.dot(d_gate_pre, gate_w.T, preferred_element_type=jnp.float32)
        + jnp.dot(d_up_pre, up_w.T, preferred_element_type=jnp.float32)
    ).astype(jnp.bfloat16)
    grad_gate_w = jnp.dot(rows_x.T, d_gate_pre, preferred_element_type=jnp.float32).astype(
        jnp.bfloat16
    )
    grad_up_w = jnp.dot(rows_x.T, d_up_pre, preferred_element_type=jnp.float32).astype(jnp.bfloat16)
    grad_down_w = jnp.dot(hidden.T, scaled, preferred_element_type=jnp.float32).astype(jnp.bfloat16)
    return (row_grad, gate_term, grad_gate_w, grad_up_w, grad_down_w)


def local(tokens, cotangent, gates, expert_ids, slots, w_gate, w_up, w_down):
    tok_rows = tokens.shape[0]
    width = tokens.shape[1]
    n_node = lax.axis_size("node")
    n_local = lax.axis_size("local")
    n_devices = n_node * n_local
    local_experts = w_gate.shape[0]
    all_experts = local_experts * n_devices
    slot_cap = 4 * tok_rows // all_experts
    per_device = local_experts * slot_cap
    position = (expert_ids * slot_cap + slots).reshape(-1)
    entries = jnp.arange(2 * tok_rows, dtype=jnp.int32)
    table = jnp.full((all_experts * slot_cap,), 2 * tok_rows, dtype=jnp.int32)
    table = table.at[position].set(entries)
    tok_ext = jnp.concatenate([tokens, jnp.zeros((1, width), jnp.bfloat16)], axis=0)
    cot_ext = jnp.concatenate([cotangent, jnp.zeros((1, width), jnp.bfloat16)], axis=0)
    gate_ext = jnp.concatenate([gates.reshape(-1), jnp.zeros((1,), jnp.bfloat16)], axis=0)
    token_row = table // 2
    send_x = jnp.take(tok_ext, token_row, axis=0)
    send_dy = jnp.take(cot_ext, token_row, axis=0)
    send_gate = jnp.take(gate_ext, table, axis=0)
    arrived_x, arrived_dy, arrived_gate = (
        lax.all_to_all(
            send_x.reshape(n_devices, per_device, width),
            ("node", "local"),
            split_axis=0,
            concat_axis=0,
            tiled=True,
        ),
        lax.all_to_all(
            send_dy.reshape(n_devices, per_device, width),
            ("node", "local"),
            split_axis=0,
            concat_axis=0,
            tiled=True,
        ),
        lax.all_to_all(
            send_gate.reshape(n_devices, per_device),
            ("node", "local"),
            split_axis=0,
            concat_axis=0,
            tiled=True,
        ),
    )
    rows_x = arrived_x.reshape(n_devices * slot_cap, width)
    rows_dy = arrived_dy.reshape(n_devices * slot_cap, width)
    rows_gate = arrived_gate.reshape(n_devices * slot_cap)
    row_grad, gate_term, grad_gate_w, grad_up_w, grad_down_w = expert_backward(
        rows_x, rows_dy, rows_gate, w_gate[0], w_up[0], w_down[0]
    )
    grad_parts = row_grad.reshape(n_devices, slot_cap, width)
    term_parts = gate_term.reshape(n_devices, slot_cap)
    gate_grads = [grad_gate_w]
    up_grads = [grad_up_w]
    down_grads = [grad_down_w]
    home_grad, home_term = (
        lax.all_to_all(grad_parts, ("node", "local"), split_axis=0, concat_axis=0, tiled=True),
        lax.all_to_all(term_parts, ("node", "local"), split_axis=0, concat_axis=0, tiled=True),
    )
    flat_grad = home_grad.reshape(all_experts * slot_cap, width)
    flat_term = home_term.reshape(all_experts * slot_cap)
    picked = jnp.take(flat_grad, position, axis=0).reshape(tok_rows, 2, width)
    grad_in = (picked[:, 0].astype(jnp.float32) + picked[:, 1].astype(jnp.float32)).astype(
        jnp.bfloat16
    )
    grad_gates = jnp.take(flat_term, position, axis=0).reshape(tok_rows, 2)
    return (
        grad_in,
        grad_gates,
        jnp.stack(gate_grads, axis=0),
        jnp.stack(up_grads, axis=0),
        jnp.stack(down_grads, axis=0),
    )


def solution(mesh):
    placed = (
        P(("node", "local"), None),
        P(("node", "local"), None),
        P(("node", "local"), None),
        P(("node", "local"), None),
        P(("node", "local"), None),
        P(("node", "local"), None, None),
        P(("node", "local"), None, None),
        P(("node", "local"), None, None),
    )
    return jax.shard_map(
        local,
        mesh=mesh,
        in_specs=placed,
        out_specs=(
            P(("node", "local"), None),
            P(("node", "local"), None),
            P(("node", "local"), None, None),
            P(("node", "local"), None, None),
            P(("node", "local"), None, None),
        ),
        check_vma=False,
    )
```

profile of v0, /device:TPU:1, one launch (start us, length us, event | category | flops | bytes accessed | tf_op | source)
XLA Modules:
  0.0 194.2 jit_solution(5970295151580027628)
XLA Ops:
  0.6 0.0 copy-start.3
  0.6 0.8 multiply_add_fusion
  1.4 0.1 copy.30
  1.5 0.1 reshape.151
  1.7 1.4 scatter_custom_fusion
  3.1 0.8 copy.31
  3.9 0.1 reshape.152
  4.1 3.5 %gather_fusion = bf16[512]{0:T(512)(128)(2,1)S(1)} fusion(bf16[257]{0:T(512)(128)(2,1)S(1)} %pad_maximum_fusion, s32[1024]{0:T(1024)S(1)} %pad_clamp_fusion.2), kind=kCustom, calls=%fused_computation.2 | custom fusion | bytes 4096 | tf_op jit(solution)/shard_map/jit(_take)/gather | solution.py:54
  7.6 0.8 select_n.75
  8.4 11.5 %all-to-all-start = ((bf16[128,1,4]{2,1,0:T(2,128)(2,1)}), bf16[128,1,4]{2,1,0:T(2,128)(2,1)S(1)}, u32[]{:S(2)}, u32[]{:S(2)}) async-start(bf16[128,1,4]{2,1,0:T(2,128)(2,1)} %select_n.75), calls=%async_computation | async-start | bytes 131072 | tf_op jit(solution)/shard_map/all_to_all | solution.py:70
  19.9 1.1 concatenate.10
  21.0 0.0 copy-done.3
  21.1 2.5 %gather_fusion.3 = bf16[512,2048]{1,0:T(8,128)(2,1)S(1)} fusion(bf16[129,2048]{1,0:T(8,128)(2,1)S(1)} %concatenate.10, s32[1024]{0:T(1024)S(1)} %pad_clamp_fusion.1), kind=kCustom, calls=%fused_computation.clone | custom fusion | bytes 4196352 | tf_op jit(solution)/shard_map/jit(_take)/gather | solution.py:53
  23.5 3.3 %gather_fusion.4 = bf16[512,2048]{1,0:T(8,128)(2,1)} fusion(bf16[129,2048]{1,0:T(8,128)(2,1)S(1)} %concatenate.11, s32[1024]{0:T(1024)S(1)} %pad_clamp_fusion.1), kind=kCustom, calls=%fused_computation.1.clone | custom fusion | bytes 4196352 | tf_op jit(solution)/shard_map/jit(_take)/gather | solution.py:52
  26.8 4.0 %broadcast_select_fusion.1 = (bf16[512,2048]{1,0:T(8,128)(2,1)}, bf16[512,2048]{1,0:T(8,128)(2,1)}) fusion(bf16[512,2048]{1,0:T(8,128)(2,1)S(1)} %gather_fusion.3, pred[512]{0:T(512)(128)(4,1)S(1)} %get-tuple-element.18, bf16[512,2048]{1,0:T(8,128)(2,1)} %gather_fusion.4), kind=kLoop, calls=%fused_computation.32 | loop fusion | flops 2097152 | bytes 8389120 | tf_op jit(solution)/shard_map/jit(_take)/select_n | solution.py:53
  30.8 4.1 %reshape.153 = bf16[128,4,2048]{2,1,0:T(4,128)(2,1)} reshape(bf16[512,2048]{1,0:T(8,128)(2,1)} %get-tuple-element.23) | data formatting | bytes 4194304 | tf_op jit(solution)/shard_map/reshape | solution.py:64
  34.9 0.0 all-to-all-done
  34.9 9.8 %all-to-all-start.1 = ((bf16[128,4,2048]{2,1,0:T(4,128)(2,1)}), bf16[128,4,2048]{2,1,0:T(4,128)(2,1)S(1)}, u32[]{:S(2)}, u32[]{:S(2)}) async-start(bf16[128,4,2048]{2,1,0:T(4,128)(2,1)} %reshape.153), calls=%async_computation.1 | async-start | bytes 4194304 | tf_op jit(solution)/shard_map/all_to_all | solution.py:63
  44.7 4.1 %reshape.154 = bf16[128,4,2048]{2,1,0:T(4,128)(2,1)} reshape(bf16[512,2048]{1,0:T(8,128)(2,1)} %get-tuple-element.24) | data formatting | bytes 4194304 | tf_op jit(solution)/shard_map/reshape | solution.py:57
  48.8 26.1 %all-to-all-done.1 = bf16[128,4,2048]{2,1,0:T(4,128)(2,1)S(1)} async-done(((bf16[128,4,2048]{2,1,0:T(4,128)(2,1)}), bf16[128,4,2048]{2,1,0:T(4,128)(2,1)S(1)}, u32[]{:S(2)}, u32[]{:S(2)}) %all-to-all-start.1) | async-done | bytes 2097184 | tf_op jit(solution)/shard_map/all_to_all | solution.py:63
  75.0 5.8 %all-to-all-start.2 = ((bf16[128,4,2048]{2,1,0:T(4,128)(2,1)}), bf16[128,4,2048]{2,1,0:T(4,128)(2,1)}, u32[]{:S(2)}, u32[]{:S(2)}) async-start(bf16[128,4,2048]{2,1,0:T(4,128)(2,1)} %reshape.154), calls=%async_computation.2 | async-start | bytes 4194304 | tf_op jit(solution)/shard_map/all_to_all | solution.py:56
  80.7 0.1 convert_element_type.106
  80.8 2.2 %multiply_convert_fusion.1 = bf16[128,4,2048]{2,1,0:T(4,128)(2,1)} fusion(f32[128,4]{1,0:T(8,128)S(1)} %bitcast.42, bf16[128,4,2048]{2,1,0:T(4,128)(2,1)S(1)} %all-to-all-done.1), kind=kLoop, calls=%fused_computation.24 | loop fusion | flops 3145728 | bytes 4196352 | tf_op jit(solution)/shard_map/convert_element_type | solution.py:14
  83.0 3.9 %convert_element_type.87 = bf16[512,2048]{1,0:T(8,128)(2,1)} reshape(bf16[128,4,2048]{2,1,0:T(4,128)(2,1)} %multiply_convert_fusion.1) | data formatting | bytes 4194304 | tf_op jit(solution)/shard_map/convert_element_type | solution.py:14
  87.0 6.5 %fusion.10 = f32[512,1024]{1,0:T(8,128)} fusion(bf16[512,2048]{1,0:T(8,128)(2,1)} %convert_element_type.87, bf16[1,1024,2048]{2,1,0:T(8,128)(2,1)} %param.17), kind=kOutput, calls=%fused_computation.16 | convolution fusion | flops 2147483648 | bytes 8388608 | tf_op jit(solution)/shard_map/dot_general | solution.py:15
  93.5 17.3 %all-to-all-done.2 = bf16[128,4,2048]{2,1,0:T(4,128)(2,1)} async-done(((bf16[128,4,2048]{2,1,0:T(4,128)(2,1)}), bf16[128,4,2048]{2,1,0:T(4,128)(2,1)}, u32[]{:S(2)}, u32[]{:S(2)}) %all-to-all-start.2) | async-done | bytes 2097184 | tf_op jit(solution)/shard_map/all_to_all | solution.py:56
  110.8 3.9 %reshape.155 = bf16[512,2048]{1,0:T(8,128)(2,1)} reshape(bf16[128,4,2048]{2,1,0:T(4,128)(2,1)} %all-to-all-done.2) | data formatting | bytes 4194304 | tf_op jit(solution)/shard_map/reshape | solution.py:78
  114.7 5.3 %fusion.2 = f32[512,1024]{1,0:T(8,128)S(1)} fusion(bf16[512,2048]{1,0:T(8,128)(2,1)} %reshape.155, bf16[1,2048,1024]{2,1,0:T(8,128)(2,1)} %param.15), kind=kOutput, calls=%fused_computation.8 | convolution fusion | flops 2147483648 | bytes 8388608 | tf_op jit(solution)/shard_map/dot_general | solution.py:8
  120.0 0.0 copy-done.1
  120.0 0.0 copy-done.4
  120.0 0.0 copy-done.10
  120.0 4.3 %multiply_convert_fusion.3 = (bf16[512,1024]{1,0:T(8,128)(2,1)S(1)}, bf16[512,1024]{1,0:T(8,128)(2,1)}, bf16[512,1024]{1,0:T(8,128)(2,1)}) fusion(f32[512,1024]{1,0:T(8,128)S(1)} %fusion.2, f32[512,1024]{1,0:T(8,128)S(1)} %copy-done.10, bf16[512,2048]{1,0:T(8,128)(2,1)S(1)} %copy-done.1, bf16[1,2048,1024]{2,1,0:T(8,128)(2,1)S(1)} %copy-done.4), kind=kOutput, calls=%fused_computation.26 | convolution fusion | flops 2155347968 | bytes 13631488 | tf_op jit(solution)/shard_map/dot_general | solution.py:9
  124.4 2.5 %reshape.160 = f32[512,2048]{1,0:T(8,128)} reshape(bf16[128,4,2048]{2,1,0:T(4,128)(2,1)S(1)} %all-to-all-done.1) | data formatting | bytes 6291456 | tf_op jit(solution)/shard_map/convert_element_type | solution.py:14
  126.9 0.0 copy-done.6
  126.9 6.0 %multiply_reduce_fusion = bf16[512]{0:T(512)(128)(2,1)S(1)} fusion(f32[512,2048]{1,0:T(8,128)} %reshape.160, bf16[512,1024]{1,0:T(8,128)(2,1)S(1)} %get-tuple-element.20, bf16[1,1024,2048]{2,1,0:T(8,128)(2,1)} %param.17), kind=kOutput, calls=%fused_computation.22 | convolution fusion | flops 2149580288 | bytes 9438208 | tf_op jit(solution)/shard_map/dot_general | solution.py:16
  132.8 0.8 convert_element_type.109
  133.6 4.7 %all-to-all-start.4 = ((bf16[128,1,4]{2,1,0:T(2,128)(2,1)}), bf16[128,1,4]{2,1,0:T(2,128)(2,1)S(1)}, u32[]{:S(2)}, u32[]{:S(2)}) async-start(bf16[128,1,4]{2,1,0:T(2,128)(2,1)} %convert_element_type.109), calls=%async_computation.4 | async-start | bytes 131072 | tf_op jit(solution)/shard_map/all_to_all | solution.py:91
  138.3 0.0 copy-done.8
  138.3 0.0 copy-start.5
  138.3 0.0 copy-start.11
  138.3 4.7 %fusion = f32[512,2048]{1,0:T(8,128)S(1)} fusion(bf16[512,1024]{1,0:T(8,128)(2,1)S(1)} %copy-done.8, bf16[1,2048,1024]{2,1,0:T(8,128)(2,1)} %param.15), kind=kOutput, calls=%fused_computation.6 | convolution fusion | flops 2147483648 | bytes 9437184 | tf_op jit(solution)/shard_map/dot_general | solution.py:23
  143.0 2.4 %add_convert_fusion = bf16[512,2048]{1,0:T(8,128)(2,1)S(1)} fusion(f32[512,2048]{1,0:T(8,128)S(1)} %fusion, bf16[512,1024]{1,0:T(8,128)(2,1)S(1)} %copy-done.11, bf16[1,2048,1024]{2,1,0:T(8,128)(2,1)S(1)} %copy-done.5), kind=kOutput, calls=%fused_computation.23 | convolution fusion | flops 2149580800 | bytes 11534336 | tf_op jit(solution)/shard_map/dot_general | solution.py:24
  145.4 2.2 %reshape.156 = bf16[128,4,2048]{2,1,0:T(4,128)(2,1)} reshape(bf16[512,2048]{1,0:T(8,128)(2,1)S(1)} %add_convert_fusion) | data formatting | bytes 4194304 | tf_op jit(solution)/shard_map/reshape | solution.py:84
  147.6 0.1 all-to-all-done.4
  147.7 10.3 %all-to-all-start.3 = ((bf16[128,4,2048]{2,1,0:T(4,128)(2,1)}), bf16[128,4,2048]{2,1,0:T(4,128)(2,1)}, u32[]{:S(2)}, u32[]{:S(2)}) async-start(bf16[128,4,2048]{2,1,0:T(4,128)(2,1)} %reshape.156), calls=%async_computation.3 | async-start | bytes 4194304 | tf_op jit(solution)/shard_map/all_to_all | solution.py:90
  158.0 0.2 convert_reduce_fusion
  158.2 0.1 reshape.161
  158.3 0.0 copy-done.2
  158.3 0.0 copy-start.9
  158.4 5.7 %convert_bitcast_fusion.1 = bf16[1,2048,1024]{2,1,0:T(8,128)(2,1)} fusion(bf16[512,2048]{1,0:T(8,128)(2,1)S(1)} %copy-done.2, bf16[512,1024]{1,0:T(8,128)(2,1)} %get-tuple-element.22), kind=kOutput, calls=%fused_computation.20 | convolution fusion | flops 2149580800 | bytes 7340032 | tf_op jit(solution)/shard_map/dot_general | solution.py:29
  164.1 4.4 %convert_bitcast_fusion.2 = bf16[1,2048,1024]{2,1,0:T(8,128)(2,1)} fusion(bf16[512,2048]{1,0:T(8,128)(2,1)S(1)} %copy-done.2, bf16[512,1024]{1,0:T(8,128)(2,1)S(1)} %copy-done.9), kind=kOutput, calls=%fused_computation.21 | convolution fusion | flops 2149580800 | bytes 7340032 | tf_op jit(solution)/shard_map/dot_general | solution.py:26
  168.5 4.5 %convert_bitcast_fusion = bf16[1,1024,2048]{2,1,0:T(8,128)(2,1)} fusion(bf16[512,1024]{1,0:T(8,128)(2,1)S(1)} %copy-done.7, f32[512,2048]{1,0:T(8,128)S(1)} %copy-done, f32[512]{0:T(512)S(1)} %reshape.161), kind=kOutput, calls=%fused_computation.18 | convolution fusion | flops 2151677952 | bytes 9439232 | tf_op jit(solution)/shard_map/dot_general | solution.py:30
  173.0 0.2 reduce
  173.2 0.1 reshape.158
  173.3 1.9 gather_fusion.2
  175.2 0.2 gather.23
  175.4 0.1 copy.35
  175.5 0.5 broadcast_select_fusion.2
  176.0 11.9 %all-to-all-done.3 = bf16[128,4,2048]{2,1,0:T(4,128)(2,1)} async-done(((bf16[128,4,2048]{2,1,0:T(4,128)(2,1)}), bf16[128,4,2048]{2,1,0:T(4,128)(2,1)}, u32[]{:S(2)}, u32[]{:S(2)}) %all-to-all-start.3) | async-done | bytes 2097184 | tf_op jit(solution)/shard_map/all_to_all | solution.py:90
  187.9 2.5 %reshape.157 = bf16[512,2048]{1,0:T(8,128)(2,1)S(1)} reshape(bf16[128,4,2048]{2,1,0:T(4,128)(2,1)} %all-to-all-done.3) | data formatting | bytes 4194304 | tf_op jit(solution)/shard_map/reshape | solution.py:93
  190.5 1.4 gather_fusion.1
  191.8 0.7 gather.21
  192.5 0.7 copy_select_fusion
  193.2 0.9 fusion.18
  (23 shorter events, 0.1 us)
Async XLA Ops:
  0.6 20.4 %copy-start.3 = (bf16[128,2048]{1,0:T(8,128)(2,1)S(1)}, bf16[128,2048]{1,0:T(8,128)(2,1)}, u32[]{:S(2)}) copy-start(bf16[128,2048]{1,0:T(8,128)(2,1)} %param.10) | copy-start | bytes 1572868
  8.4 26.6 %all-to-all-start = ((bf16[128,1,4]{2,1,0:T(2,128)(2,1)}), bf16[128,1,4]{2,1,0:T(2,128)(2,1)S(1)}, u32[]{:S(2)}, u32[]{:S(2)}) async-start(bf16[128,1,4]{2,1,0:T(2,128)(2,1)} %select_n.75), calls=%async_computation | async-start | bytes 131072 | tf_op jit(solution)/shard_map/all_to_all | solution.py:70
  34.9 40.0 %all-to-all-start.1 = ((bf16[128,4,2048]{2,1,0:T(4,128)(2,1)}), bf16[128,4,2048]{2,1,0:T(4,128)(2,1)S(1)}, u32[]{:S(2)}, u32[]{:S(2)}) async-start(bf16[128,4,2048]{2,1,0:T(4,128)(2,1)} %reshape.153), calls=%async_computation.1 | async-start | bytes 4194304 | tf_op jit(solution)/shard_map/all_to_all | solution.py:63
  75.0 35.8 %all-to-all-start.2 = ((bf16[128,4,2048]{2,1,0:T(4,128)(2,1)}), bf16[128,4,2048]{2,1,0:T(4,128)(2,1)}, u32[]{:S(2)}, u32[]{:S(2)}) async-start(bf16[128,4,2048]{2,1,0:T(4,128)(2,1)} %reshape.154), calls=%async_computation.2 | async-start | bytes 4194304 | tf_op jit(solution)/shard_map/all_to_all | solution.py:56
  114.7 5.3 %copy-start.1 = (bf16[512,2048]{1,0:T(8,128)(2,1)S(1)}, bf16[512,2048]{1,0:T(8,128)(2,1)}, u32[]{:S(2)}) copy-start(bf16[512,2048]{1,0:T(8,128)(2,1)} %reshape.155) | copy-start | bytes 6291460
  114.7 5.3 %copy-start.4 = (bf16[1,2048,1024]{2,1,0:T(8,128)(2,1)S(1)}, bf16[1,2048,1024]{2,1,0:T(8,128)(2,1)}, u32[]{:S(2)}) copy-start(bf16[1,2048,1024]{2,1,0:T(8,128)(2,1)} %param.16) | copy-start | bytes 12582916
  114.7 5.3 %copy-start.10 = (f32[512,1024]{1,0:T(8,128)S(1)}, f32[512,1024]{1,0:T(8,128)}, u32[]{:S(2)}) copy-start(f32[512,1024]{1,0:T(8,128)} %fusion.10) | copy-start | bytes 6291460
  124.4 2.5 %copy-start.6 = (bf16[512,1024]{1,0:T(8,128)(2,1)}, bf16[512,1024]{1,0:T(8,128)(2,1)S(1)}, u32[]{:S(2)}) copy-start(bf16[512,1024]{1,0:T(8,128)(2,1)S(1)} %get-tuple-element.20) | copy-start | bytes 3145732
  126.9 11.4 %copy-start.8 = (bf16[512,1024]{1,0:T(8,128)(2,1)S(1)}, bf16[512,1024]{1,0:T(8,128)(2,1)}, u32[]{:S(2)}) copy-start(bf16[512,1024]{1,0:T(8,128)(2,1)} %get-tuple-element.21) | copy-start | bytes 3145732
  133.6 14.1 %all-to-all-start.4 = ((bf16[128,1,4]{2,1,0:T(2,128)(2,1)}), bf16[128,1,4]{2,1,0:T(2,128)(2,1)S(1)}, u32[]{:S(2)}, u32[]{:S(2)}) async-start(bf16[128,1,4]{2,1,0:T(2,128)(2,1)} %convert_element_type.109), calls=%async_computation.4 | async-start | bytes 131072 | tf_op jit(solution)/shard_map/all_to_all | solution.py:91
  138.3 4.7 %copy-start.5 = (bf16[1,2048,1024]{2,1,0:T(8,128)(2,1)S(1)}, bf16[1,2048,1024]{2,1,0:T(8,128)(2,1)}, u32[]{:S(2)}) copy-start(bf16[1,2048,1024]{2,1,0:T(8,128)(2,1)} %param.16) | copy-start | bytes 12582916
  138.3 4.7 %copy-start.11 = (bf16[512,1024]{1,0:T(8,128)(2,1)S(1)}, bf16[512,1024]{1,0:T(8,128)(2,1)}, u32[]{:S(2)}) copy-start(bf16[512,1024]{1,0:T(8,128)(2,1)} %get-tuple-element.22) | copy-start | bytes 3145732
  147.6 10.7 %copy-start.2 = (bf16[512,2048]{1,0:T(8,128)(2,1)S(1)}, bf16[512,2048]{1,0:T(8,128)(2,1)}, u32[]{:S(2)}) copy-start(bf16[512,2048]{1,0:T(8,128)(2,1)} %reshape.155) | copy-start | bytes 6291460
  147.7 40.2 %all-to-all-start.3 = ((bf16[128,4,2048]{2,1,0:T(4,128)(2,1)}), bf16[128,4,2048]{2,1,0:T(4,128)(2,1)}, u32[]{:S(2)}, u32[]{:S(2)}) async-start(bf16[128,4,2048]{2,1,0:T(4,128)(2,1)} %reshape.156), calls=%async_computation.3 | async-start | bytes 4194304 | tf_op jit(solution)/shard_map/all_to_all | solution.py:90
  158.3 5.7 %copy-start.9 = (bf16[512,1024]{1,0:T(8,128)(2,1)S(1)}, bf16[512,1024]{1,0:T(8,128)(2,1)}, u32[]{:S(2)}) copy-start(bf16[512,1024]{1,0:T(8,128)(2,1)} %get-tuple-element.21) | copy-start | bytes 3145732
  164.1 4.4 %copy-start = (f32[512,2048]{1,0:T(8,128)S(1)}, f32[512,2048]{1,0:T(8,128)}, u32[]{:S(2)}) copy-start(f32[512,2048]{1,0:T(8,128)} %reshape.160) | copy-start | bytes 12582916
  164.1 4.4 %copy-start.7 = (bf16[512,1024]{1,0:T(8,128)(2,1)S(1)}, bf16[512,1024]{1,0:T(8,128)(2,1)}, u32[]{:S(2)}) copy-start(bf16[512,1024]{1,0:T(8,128)(2,1)} %copy-done.6) | copy-start | bytes 3145732
where the time goes:
time: 195 us; the launch traced here: 194 us
  waiting for transfers between devices  55.4 us (28%)
  matrix products  43.8 us (22%)
  local copies, waits for them, and re-layouts  42.3 us (22%)
  starting transfers between devices  42 us (22%)
  other arithmetic  9.67 us (5%)
    all_to_all x1, waiting for transfers between devices, local(): lax.all_to_all(send_dy.reshape(n_devices, per_device, width), ('node', 'l...  26.1 us
    all_to_all x1, waiting for transfers between devices, local(): lax.all_to_all(send_x.reshape(n_devices, per_device, width), ('node', 'lo...  17.3 us
    all_to_all x1, waiting for transfers between devices, local(): lax.all_to_all(grad_parts, ('node', 'local'), split_axis=0, concat_axis=0...  11.9 us
    all_to_all x1, starting transfers between devices, local(): lax.all_to_all(send_gate.reshape(n_devices, per_device), ('node', 'local'...  11.5 us
    all_to_all x1, starting transfers between devices, local(): lax.all_to_all(grad_parts, ('node', 'local'), split_axis=0, concat_axis=0...  10.3 us
    all_to_all x1, starting transfers between devices, local(): lax.all_to_all(send_dy.reshape(n_devices, per_device, width), ('node', 'l...  9.76 us
    dot_general x1, matrix products, expert_backward(): d_hidden = jnp.dot(scaled, down_w.T, preferred_element_type=jnp.float32)  6.5 us
    dot_general x1, matrix products, expert_backward(): expert_out = jnp.dot(hidden, down_w, preferred_element_type=jnp.float32)  5.96 us
  transfers between devices with their start and end apart: 5, of which 4 were waited for; matrix products, arithmetic and copies ran while one was open for 30% of the time, Pallas kernels for 0%

commit v1 on v0

v1 whole, which is shorter than its diff:
```python
import functools

import jax
import jax.numpy as jnp
from jax import lax
from jax.experimental import pallas as pl
from jax.experimental.pallas import tpu as pltpu
from jax.sharding import PartitionSpec as P

MESH = pl.DeviceIdType.MESH
BF = jnp.bfloat16
F32 = jnp.float32
LANES = 128
NT = (((1,), (1,)), ((), ()))
TN = (((0,), (0,)), ((), ()))


def iota(shape, dim):
    return lax.broadcasted_iota(jnp.int32, shape, dim)


def layer_kernel(
    dims,
    ids_ref, slots_ref, gates_ref, tok_ref, cot_ref, wg_hbm, wu_hbm, wd_hbm,
    gin_ref, ggate_ref, xs_hbm, hid_hbm, dg_hbm, du_hbm,
    wg, wu, wd, gx, gs, bk, ms, mr, s1, r1, pk, s2, r2, hid, dg, du, s3, r3, s4, r4,
    w_sem, out_sem, n_send, n_recv, m_send, m_recv, z_send, z_recv, b_send, b_recv, h_send, h_recv,
):
    Y, X, L, RG, CAP, D, H = dims
    NG = Y * X
    NP = NG * RG
    TOK = tok_ref.shape[0]
    XC = X * CAP
    XR = X * RG
    ROWS = L * XC
    DR = D + LANES
    n = lax.axis_index("node")
    l = lax.axis_index("local")
    y = n // X
    x = lax.rem(n, X)

    def node_of(yy, xx):
        return lax.rem(yy + Y, Y) * X + lax.rem(xx + X, X)

    barrier = pltpu.get_barrier_semaphore()
    for k in range(Y):
        for dx in range(X):
            if k or dx:
                pl.semaphore_signal(
                    barrier, inc=1, device_id=(node_of(y + k, x + dx), l), device_id_type=MESH
                )
    for d in range(1, L):
        pl.semaphore_signal(barrier, inc=1, device_id=(n, lax.rem(l + d, L)), device_id_type=MESH)

    loads = [
        pltpu.make_async_copy(src.at[0], dst, w_sem.at[i])
        for i, (src, dst) in enumerate(((wg_hbm, wg), (wu_hbm, wu), (wd_hbm, wd)))
    ]
    for load in loads:
        load.start()

    e = ids_ref[...]
    s = slots_ref[...]
    gate = gates_ref[...].astype(F32)
    grp = e // L
    gi = iota((NG, TOK), 0)
    o0 = (grp[0:1] == gi).astype(F32)
    o1 = (grp[1:2] == gi).astype(F32)
    tri = (iota((TOK, TOK), 0) < iota((TOK, TOK), 1)).astype(F32).astype(BF)
    c0 = jnp.dot(o0.astype(BF), tri, preferred_element_type=F32)
    c1 = jnp.dot(o1.astype(BF), tri, preferred_element_type=F32)
    total0 = jnp.sum(o0, axis=1, keepdims=True)
    rank0 = jnp.sum(o0 * c0, axis=0, keepdims=True)
    rank1 = jnp.sum(o1 * (c1 + total0), axis=0, keepdims=True)
    pos0 = (grp[0:1] * RG).astype(F32) + rank0
    pos1 = (grp[1:2] * RG).astype(F32) + rank1
    pi = iota((NP, TOK), 0).astype(F32)
    b0 = (pi == pos0).astype(F32)
    b1 = (pi == pos1).astype(F32)
    gx[...] = (b0 + b1).astype(BF)
    gs[...] = (b0 * gate[0:1] + b1 * gate[1:2]).astype(BF)
    bk[0] = b0.astype(BF)
    bk[1] = b1.astype(BF)

    v = (e - grp * L) * XC + x * CAP + s
    v0 = jnp.broadcast_to(v[0:1], (8, TOK)).astype(F32).astype(BF)
    v1 = jnp.broadcast_to(v[1:2], (8, TOK)).astype(F32).astype(BF)
    val = lax.dot_general(v0, bk[0], NT, preferred_element_type=F32) + lax.dot_general(
        v1, bk[1], NT, preferred_element_type=F32
    )
    own = (iota((NG, NP), 1) // RG == iota((NG, NP), 0)).astype(F32)
    pp = iota((NP, LANES), 0)
    pick = (iota((NP, LANES), 1) == x * RG + lax.rem(pp, RG)).astype(F32).astype(BF)
    meta = jnp.dot((own * val[0:1]).astype(BF), pick, preferred_element_type=F32)
    for g in range(NG):
        ms[g] = jnp.broadcast_to(meta[g : g + 1], (8, LANES))

    def row_copy(k, dx):
        g = node_of(y - k, x + dx)
        return pltpu.make_async_remote_copy(
            s1.at[g], r1.at[k, x], n_send.at[k, dx], n_recv.at[k, dx],
            device_id=(g, l), device_id_type=MESH,
        )

    def meta_copy(k, dx):
        g = node_of(y - k, x + dx)
        return pltpu.make_async_remote_copy(
            ms.at[g], mr.at[k, x], m_send.at[k, dx], m_recv.at[k, dx],
            device_id=(g, l), device_id_type=MESH,
        )

    def row_arrival(k, dx):
        xs = lax.rem(x - dx + X, X)
        return pltpu.make_async_remote_copy(
            s1.at[n], r1.at[k, xs], n_send.at[k, dx], n_recv.at[k, dx],
            device_id=(node_of(y + k, xs), l), device_id_type=MESH,
        )

    def meta_arrival(k, dx):
        xs = lax.rem(x - dx + X, X)
        return pltpu.make_async_remote_copy(
            ms.at[n], mr.at[k, xs], m_send.at[k, dx], m_recv.at[k, dx],
            device_id=(node_of(y + k, xs), l), device_id_type=MESH,
        )

    def z_copy(k, d):
        j = lax.rem(l + d, L)
        return pltpu.make_async_remote_copy(
            s2.at[k, j], r2.at[k, l], z_send.at[k, d], z_recv.at[k, d],
            device_id=(n, j), device_id_type=MESH,
        )

    def z_arrival(k, d):
        j = lax.rem(l - d + L, L)
        return pltpu.make_async_remote_copy(
            s2.at[k, j], r2.at[k, j], z_send.at[k, d], z_recv.at[k, d],
            device_id=(n, j), device_id_type=MESH,
        )

    def b_copy(k, d):
        j = lax.rem(l + d, L)
        return pltpu.make_async_remote_copy(
            s3.at[k, j], r3.at[k, l], b_send.at[k, d], b_recv.at[k, d],
            device_id=(n, j), device_id_type=MESH,
        )

    def b_arrival(k, d):
        j = lax.rem(l - d + L, L)
        return pltpu.make_async_remote_copy(
            s3.at[k, j], r3.at[k, j], b_send.at[k, d], b_recv.at[k, d],
            device_id=(n, j), device_id_type=MESH,
        )

    def home_copy(k, dx):
        xs = lax.rem(x + dx, X)
        return pltpu.make_async_remote_copy(
            s4.at[k, xs], r4.at[n], h_send.at[k, dx], h_recv.at[k, dx],
            device_id=(node_of(y + k, xs), l), device_id_type=MESH,
        )

    def home_arrival(k, dx):
        g = node_of(y - k, x - dx)
        return pltpu.make_async_remote_copy(
            s4.at[k, x], r4.at[g], h_send.at[k, dx], h_recv.at[k, dx],
            device_id=(g, l), device_id_type=MESH,
        )

    def tiles(width, tile, body):
        def step(i, carry):
            body(pl.multiple_of(i * tile, tile))
            return carry

        lax.fori_loop(0, width // tile, step, 0)

    td = min(512, D)
    th = min(256, H)

    def node_send(k):
        yy = lax.rem(y - k + Y, Y)
        rows = pl.ds(pl.multiple_of(yy * XR, XR), XR)
        groups = pl.ds(yy * X, X)

        def body(c):
            a = jnp.dot(gx[rows, :], tok_ref[:, pl.ds(c, td)], preferred_element_type=F32)
            s1[groups, :, pl.ds(c, td)] = a.astype(BF).reshape(X, RG, td)
            b = jnp.dot(gs[rows, :], cot_ref[:, pl.ds(c, td)], preferred_element_type=F32)
            s1[groups, :, pl.ds(c + D, td)] = b.astype(BF).reshape(X, RG, td)

        tiles(D, td, body)
        if k == 0:
            pl.semaphore_wait(barrier, NG + L - 2)
        for dx in range(X):
            if k or dx:
                meta_copy(k, dx).start()
                row_copy(k, dx).start()
            else:
                r1[0, x] = s1[n]
                mr[0, x] = ms[n]

    def z_step(k):
        for dx in range(X):
            if k or dx:
                meta_arrival(k, dx).wait_recv()
                row_arrival(k, dx).wait_recv()
        target = mr[k, 0]
        for xs in range(1, X):
            target = target + mr[k, xs]
        place = iota((ROWS, XR), 0).astype(F32) == target[0:1, :XR]
        pk[k] = place.astype(F32)
        perm = place.astype(F32).astype(BF)

        def body(c):
            rows = r1[k, :, :, pl.ds(c, td)].reshape(XR, td)
            a = jnp.dot(perm, rows, preferred_element_type=F32)
            s2[k, :, :, pl.ds(c, td)] = a.astype(BF).reshape(L, XC, td)

        tiles(2 * D, td, body)
        for d in range(1, L):
            z_copy(k, d).start()
        r2[k, l] = s2[k, l]

    saves = []

    def compute(k):
        for d in range(1, L):
            z_arrival(k, d).wait_recv()
        if k == 0:
            for load in loads:
                load.wait()

        def fwd(i, u):
            c = pl.multiple_of(i * th, th)
            xr = r2[k, :, :, 0:D].reshape(ROWS, D)
            sr = r2[k, :, :, D : 2 * D].reshape(ROWS, D)
            gp = jnp.dot(xr, wg[:, pl.ds(c, th)], preferred_element_type=F32)
            up = jnp.dot(xr, wu[:, pl.ds(c, th)], preferred_element_type=F32)
            dh = lax.dot_general(sr, wd[pl.ds(c, th), :], NT, preferred_element_type=F32)
            sig = jax.nn.sigmoid(gp)
            act = gp * sig
            hf = act * up
            hid[k, :, pl.ds(c, th)] = hf.astype(BF)
            dg[k, :, pl.ds(c, th)] = (dh * up * sig * (1.0 + gp * (1.0 - sig))).astype(BF)
            du[k, :, pl.ds(c, th)] = (dh * act).astype(BF)
            return u + jnp.sum(hf * dh, axis=1, keepdims=True)

        u = lax.fori_loop(0, H // th, fwd, jnp.zeros((ROWS, 1), F32))

        def bwd(c):
            a = lax.dot_general(dg[k], wg[pl.ds(c, th), :], NT, preferred_element_type=F32)
            a = a + lax.dot_general(du[k], wu[pl.ds(c, th), :], NT, preferred_element_type=F32)
            s3[k, :, :, pl.ds(c, th)] = a.astype(BF).reshape(L, XC, th)

        tiles(D, th, bwd)
        hi = u.astype(BF).astype(F32)
        col = iota((ROWS, LANES), 1)
        both = jnp.where(col == 0, hi, jnp.where(col == 1, u - hi, 0.0))
        s3[k, :, :, D:DR] = both.astype(BF).reshape(L, XC, LANES)
        for i, (src, dst) in enumerate(((r2, xs_hbm), (hid, hid_hbm), (dg, dg_hbm), (du, du_hbm))):
            save = pltpu.make_async_copy(src.at[k], dst.at[k], out_sem.at[k, i])
            save.start()
            saves.append(save)

    def back_send(k):
        for d in range(1, L):
            b_copy(k, d).start()
        r3[k, l] = s3[k, l]

    def home_step(k):
        for d in range(1, L):
            b_arrival(k, d).wait_recv()
        perm = pk[k].T.astype(BF)
        t3 = DR // 17 if DR % 17 == 0 else LANES

        def body(c):
            rows = r3[k, :, :, pl.ds(c, td)].reshape(ROWS, td)
            a = jnp.dot(perm, rows, preferred_element_type=F32)
            s4[k, :, :, pl.ds(c, td)] = a.astype(BF).reshape(X, RG, td)

        tiles(D, td, body)
        a = jnp.dot(perm, r3[k, :, :, D:DR].reshape(ROWS, LANES), preferred_element_type=F32)
        s4[k, :, :, D:DR] = a.astype(BF).reshape(X, RG, LANES)
        for dx in range(X):
            if k or dx:
                home_copy(k, dx).start()
            else:
                r4[n] = s4[0, x]

    for k in range(Y):
        node_send(k)
    order = [("z", 0), ("z", 1)]
    for k in range(Y):
        order.append(("c", k))
        if k + 2 < Y:
            order.append(("z", k + 2))
    for what, k in order:
        if what == "z":
            z_step(k)
        else:
            compute(k)
            if k == Y - 1:
                pass
            back_send(k)
    for k in range(Y):
        home_step(k)

    for k in range(Y):
        for dx in range(X):
            if k or dx:
                home_arrival(k, dx).wait_recv()
    collect = gx[...].astype(F32).T.astype(BF)

    def body(c):
        rows = r4[:, :, pl.ds(c, td)].reshape(NP, td)
        gin_ref[:, pl.ds(c, td)] = jnp.dot(collect, rows, preferred_element_type=F32).astype(BF)

    tiles(D, td, body)
    sums = r4[:, :, D:DR].reshape(NP, LANES).astype(F32).T.astype(BF)
    for k in range(2):
        t = jnp.dot(sums, bk[k], preferred_element_type=F32)
        ggate_ref[k : k + 1, :] = ((t[0:1] + t[1:2]) / gate[k : k + 1]).astype(BF)

    for save in saves:
        save.wait()
    for k in range(Y):
        for dx in range(X):
            if k or dx:
                meta_copy(k, dx).wait_send()
                row_copy(k, dx).wait_send()
                home_copy(k, dx).wait_send()
        for d in range(1, L):
            z_copy(k, d).wait_send()
            b_copy(k, d).wait_send()


def weights_kernel(x_ref, sc_ref, hid_ref, dg_ref, du_ref, og_ref, ou_ref, od_ref):
    rows = x_ref.shape[0] * x_ref.shape[1]
    xt = x_ref[...].reshape(rows, -1)
    a = dg_ref[...].reshape(rows, -1)
    og_ref[0] = lax.dot_general(xt, a, TN, preferred_element_type=F32).astype(BF)
    b = du_ref[...].reshape(rows, -1)
    ou_ref[0] = lax.dot_general(xt, b, TN, preferred_element_type=F32).astype(BF)
    h = hid_ref[...].reshape(rows, -1)
    c = sc_ref[...].reshape(rows, -1)
    od_ref[0] = lax.dot_general(h, c, TN, preferred_element_type=F32).astype(BF)


def local(grid_y, tokens, cotangent, gates, expert_ids, slots, w_gate, w_up, w_down):
    tok, width = tokens.shape
    hidden = w_gate.shape[2]
    n_node = lax.axis_size("node")
    n_local = lax.axis_size("local")
    Y, X, L = grid_y, n_node // grid_y, n_local
    cap = 4 * tok // (n_node * n_local)
    RG = 2 * tok // n_node
    D, H = width, hidden
    XC, XR, ROWS, NP, DR = X * cap, X * RG, L * X * cap, 2 * tok, width + LANES
    vmem = pl.BlockSpec(memory_space=pltpu.VMEM)
    hbm = pl.BlockSpec(memory_space=pl.ANY)
    sem = pltpu.SemaphoreType.DMA
    shape = jax.ShapeDtypeStruct
    macs = 5 * Y * ROWS * D * H
    gin, ggate, xs, hid, dg, du = pl.pallas_call(
        functools.partial(layer_kernel, (Y, X, L, RG, cap, D, H)),
        out_shape=(
            shape((tok, D), BF),
            shape((2, tok), BF),
            shape((Y, L, XC, 2 * D), BF),
            shape((Y, ROWS, H), BF),
            shape((Y, ROWS, H), BF),
            shape((Y, ROWS, H), BF),
        ),
        in_specs=[vmem] * 5 + [hbm] * 3,
        out_specs=(vmem, vmem, hbm, hbm, hbm, hbm),
        scratch_shapes=[
            pltpu.VMEM((D, H), BF),
            pltpu.VMEM((D, H), BF),
            pltpu.VMEM((H, D), BF),
            pltpu.VMEM((NP, tok), BF),
            pltpu.VMEM((NP, tok), BF),
            pltpu.VMEM((2, NP, tok), BF),
            pltpu.VMEM((n_node, 8, LANES), F32),
            pltpu.VMEM((Y, X, 8, LANES), F32),
            pltpu.VMEM((n_node, RG, 2 * D), BF),
            pltpu.VMEM((Y, X, RG, 2 * D), BF),
            pltpu.VMEM((Y, ROWS, XR), F32),
            pltpu.VMEM((Y, L, XC, 2 * D), BF),
            pltpu.VMEM((Y, L, XC, 2 * D), BF),
            pltpu.VMEM((Y, ROWS, H), BF),
            pltpu.VMEM((Y, ROWS, H), BF),
            pltpu.VMEM((Y, ROWS, H), BF),
            pltpu.VMEM((Y, L, XC, DR), BF),
            pltpu.VMEM((Y, L, XC, DR), BF),
            pltpu.VMEM((Y, X, RG, DR), BF),
            pltpu.VMEM((n_node, RG, DR), BF),
            sem((3,)),
            sem((Y, 4)),
            sem((Y, X)),
            sem((Y, X)),
            sem((Y, X)),
            sem((Y, X)),
            sem((Y, L)),
            sem((Y, L)),
            sem((Y, L)),
            sem((Y, L)),
            sem((Y, X)),
            sem((Y, X)),
        ],
        compiler_params=pltpu.CompilerParams(
            collective_id=0, has_side_effects=True, vmem_limit_bytes=54 * 2**20
        ),
        cost_estimate=pl.CostEstimate(
            flops=2 * macs, bytes_accessed=24 * 2**20, transcendentals=Y * ROWS * H
        ),
        name="routed_layer",
    )(expert_ids.T, slots.T, gates.T, tokens, cotangent, w_gate, w_up, w_down)
    xs = xs.reshape(Y, ROWS, 2 * D)
    steps = 8
    bd, bh = D // steps, H // steps
    whole = lambda shape: pl.BlockSpec(shape, lambda i: (0, 0, 0))
    gg, gu, gd = pl.pallas_call(
        weights_kernel,
        grid=(steps,),
        out_shape=(shape((1, D, H), BF), shape((1, D, H), BF), shape((1, H, D), BF)),
        in_specs=[
            pl.BlockSpec((Y, ROWS, bd), lambda i: (0, 0, i)),
            pl.BlockSpec((Y, ROWS, D), lambda i: (0, 0, 1)),
            pl.BlockSpec((Y, ROWS, bh), lambda i: (0, 0, i)),
            whole((Y, ROWS, H)),
            whole((Y, ROWS, H)),
        ],
        out_specs=(
            pl.BlockSpec((1, bd, H), lambda i: (0, i, 0)),
            pl.BlockSpec((1, bd, H), lambda i: (0, i, 0)),
            pl.BlockSpec((1, bh, D), lambda i: (0, i, 0)),
        ),
        compiler_params=pltpu.CompilerParams(vmem_limit_bytes=48 * 2**20),
        cost_estimate=pl.CostEstimate(
            flops=6 * Y * ROWS * D * H, bytes_accessed=20 * 2**20, transcendentals=0
        ),
        name="weight_grads",
    )(xs, xs, hid, dg, du)
    return gin, ggate.T, gg, gu, gd


def solution(mesh):
    both = ("node", "local")
    n_node = mesh.shape["node"]
    grid_y = 1
    while (2 * grid_y) ** 2 <= n_node and n_node % (2 * grid_y) == 0:
        grid_y *= 2
    placed = (P(both, None),) * 5 + (P(both, None, None),) * 3
    return jax.shard_map(
        functools.partial(local, grid_y),
        mesh=mesh,
        in_specs=placed,
        out_specs=(P(both, None),) * 2 + (P(both, None, None),) * 3,
        check_vma=False,
    )
```

time: 195 us -> 127 us (0.65)
  Pallas kernels: 0 us -> 120 us
  waiting for transfers between devices: 55.4 us -> 0 us
  matrix products: 43.8 us -> 0 us
  starting transfers between devices: 42 us -> 0 us
  local copies, waits for them, and re-layouts: 42.3 us -> 4.98 us
  other arithmetic: 9.67 us -> 0 us
    pallas_call x0 -> x2, Pallas kernels: none -> 120 us  [the longest x1 109 us: local(): pl.pallas_call(functools.partial(layer_kernel, (Y, X, L, RG, cap, D, H)),...]
    all_to_all x5 -> x0, waiting for transfers between devices: 55.4 us -> none  [the longest x1 26.1 us: local(): lax.all_to_all(send_dy.reshape(n_devices, per_device, width), ('node', 'l...]
    dot_general x9 -> x0, matrix products: 43.8 us -> none  [the longest x1 6.5 us: expert_backward(): d_hidden = jnp.dot(scaled, down_w.T, preferred_element_type=jnp.float32)]
    all_to_all x5 -> x0, starting transfers between devices: 42 us -> none  [the longest x1 11.5 us: local(): lax.all_to_all(send_gate.reshape(n_devices, per_device), ('node', 'local'...]
    reshape x8 -> x0, local copies, waits for them, and re-layouts: 17.3 us -> none  [the longest x1 4.1 us: local(): send_x.reshape(n_devices, per_device, width)]
    gather x8 -> x0, local copies, waits for them, and re-layouts: 13.5 us -> none  [the longest x1 3.51 us: local(): send_gate = jnp.take(gate_ext, table, axis=0)]
    convert_element_type x4 -> x0, local copies, waits for them, and re-layouts: 7.31 us -> none  [the longest x1 3.94 us: expert_backward(): (gate_value[:, None] * rows_dy.astype(jnp.float32)).astype(jnp.bfloat16)]
    select_n x6 -> x0, other arithmetic: 5.28 us -> none  [the longest x1 4.04 us: local(): send_dy = jnp.take(cot_ext, token_row, axis=0)]
  transfers between devices with their start and end apart: 5 -> 0, of which waited for: 4 -> 0; matrix products, arithmetic and copies ran while one was open for 30% -> 0% of each run, Pallas kernels for 0% -> 0%
where the time goes in v1:
time: 127 us; the launch traced here: 126 us
  Pallas kernels  120 us (94%)
  local copies, waits for them, and re-layouts  4.98 us (4%)
    pallas_call x1, Pallas kernels, local(): pl.pallas_call(functools.partial(layer_kernel, (Y, X, L, RG, cap, D, H)),...  109 us
    pallas_call x1, Pallas kernels, local(): pl.pallas_call(weights_kernel, grid=(steps,), out_shape=(shape((1, D, H),...  11.1 us
    unnamed x12, local copies, waits for them, and re-layouts  4.98 us

profile of v1, /device:TPU:1, one launch (start us, length us, event | category | flops | bytes accessed | tf_op | source)
XLA Modules:
  0.0 126.1 jit_solution(17834039420601425041)
XLA Ops:
  0.6 109.3 %routed_layer.1 = (bf16[128,2048]{1,0:T(8,128)(2,1)}, bf16[2,128]{1,0:T(2,128)(2,1)}, bf16[4,8,16,4096]{3,2,1,0:T(8,128)(2,1)}, bf16[4,128,1024]{2,1,0:T(8,128)(...) custom-call(s32[2,128]{1,0:T(2,128)} %bitcast.5, s32[2,128]{1,0:T(2,128)} %bitcast.6, ...), custom_call_target="tpu_custom_call" | custom-call | flops 10737418240 | bytes 25165824 | tf_op jit(solution)/shard_map/routed_layer/pallas_call | solution.py:362
  110.0 0.0 copy-start
  110.0 1.2 copy-done
  111.2 0.0 copy-start.1
  111.2 1.2 copy-done.1
  112.4 0.0 copy-start.2
  112.4 1.2 copy-done.2
  113.6 0.0 copy-start.3
  113.6 0.0 copy-start.4
  113.6 11.1 %weight_grads.1 = (bf16[1,2048,1024]{2,1,0:T(8,128)(2,1)}, bf16[1,2048,1024]{2,1,0:T(8,128)(2,1)}, bf16[1,1024,2048]{2,1,0:T(8,128)(2,1)}) custom-call(bf16[4,128,4096]{2,1,0:T(8,128)(2,1)} %bitcast.8, bf16[4,128,4096]{2,1,0:T(8,128)(2,1)} %bitcast.9, bf16[4,128,1024]{2,1,0:T(8,128)(2,1)S(1)} %copy-done, bf16[4,128,1024]{2,1,0:T(8,128)(2,1)S(1)} %copy-done.1, ...), custom_call_target="tpu_custom_call" | custom-call | flops 6442450944 | bytes 20971520 | tf_op jit(solution)/shard_map/weight_grads/pallas_call | solution.py:420
  124.8 0.0 copy-done.3
  124.8 0.8 copy.15
  125.6 0.0 copy-done.4
  125.6 0.5 copy.16
Async XLA Ops:
  110.0 1.2 copy-start
  111.2 1.2 copy-start.1
  112.4 1.2 copy-start.2
  113.6 11.1 %copy-start.3 = (bf16[128,2048]{1,0:T(8,128)(2,1)S(1)}, bf16[128,2048]{1,0:T(8,128)(2,1)}, u32[]{:S(2)}) copy-start(bf16[128,2048]{1,0:T(8,128)(2,1)} %get-tuple-element.28) | copy-start | bytes 1572868
  113.6 11.9 %copy-start.4 = (bf16[2,128]{1,0:T(2,128)(2,1)S(1)}, bf16[2,128]{1,0:T(2,128)(2,1)}, u32[]{:S(2)}) copy-start(bf16[2,128]{1,0:T(2,128)(2,1)} %get-tuple-element.15) | copy-start | bytes 1540

commit v2 on v1

v2 whole, which is shorter than its diff:
```python
import functools

import jax
import jax.numpy as jnp
from jax import lax
from jax.experimental import pallas as pl
from jax.experimental.pallas import tpu as pltpu
from jax.sharding import PartitionSpec as P

MESH = pl.DeviceIdType.MESH
BF = jnp.bfloat16
F32 = jnp.float32
LANES = 128
PLAN = (
    "t0", "n0", "n1", "n2", "n3", "z0", "f0", "z1", "g0", "z2", "c0", "z3", "b0", "k0", "c1",
    "b1", "k1", "c2", "k2", "w3", "b2", "c3", "b3", "k3", "h0", "h1", "h2", "h3",
)
NT = (((1,), (1,)), ((), ()))
TN = (((0,), (0,)), ((), ()))


def iota(shape, dim):
    return lax.broadcasted_iota(jnp.int32, shape, dim)


def layer_kernel(
    dims,
    ids_ref, slots_ref, gates_ref, tok_hbm, cot_hbm, wg_hbm, wu_hbm, wd_hbm,
    r4, bk, sc_hbm, xt_hbm, ht_hbm, dg_hbm, du_hbm,
    tok_ref, cot_ref, wg, wu, wd, gx, gs, ms, mr, s1, r1, pk, s2, r2, xt, ht, dg, du, s3, r3, s4,
    tb, ms2, mb, oh, sb, rb,
    w_sem, out_sem, n_send, n_recv, m_send, m_recv, z_send, z_recv, b_send, b_recv, h_send, h_recv,
    t_send, t_recv, f_send, f_recv, i_send, i_recv, g_send, g_recv,
):
    Y, X, L, RG, CAP, D, H = dims
    NG = Y * X
    NP = NG * RG
    TOK = tok_hbm.shape[0]
    XC = X * CAP
    XR = X * RG
    ROWS = L * XC
    DR = D + LANES
    BW = D // 2
    AW = 2 * D - BW
    Z = L // 2
    LC = L * CAP
    n = lax.axis_index("node")
    l = lax.axis_index("local")
    core = lax.rem(l, 2)
    zz = l // 2
    y = n // X
    x = lax.rem(n, X)
    offset = [0] + [o for i in range(1, Y // 2 + 1) for o in sorted({i, Y - i})]

    def node_of(yy, xx):
        return lax.rem(yy + Y, Y) * X + lax.rem(xx + X, X)

    barrier = pltpu.get_barrier_semaphore()
    for k in range(Y):
        for dx in range(X):
            if k or dx:
                pl.semaphore_signal(
                    barrier, inc=1, device_id=(node_of(y + k, x + dx), l), device_id_type=MESH
                )
    for d in range(1, L):
        pl.semaphore_signal(barrier, inc=1, device_id=(n, lax.rem(l + d, L)), device_id_type=MESH)

    loads = [
        pltpu.make_async_copy(src.at[0], dst, w_sem.at[i])
        for i, (src, dst) in enumerate(((wg_hbm, wg), (wu_hbm, wu), (wd_hbm, wd)))
    ]
    rows_in = [
        pltpu.make_async_copy(src, dst, w_sem.at[3 + i])
        for i, (src, dst) in enumerate(((tok_hbm, tok_ref), (cot_hbm, cot_ref)))
    ]
    for load in rows_in:
        load.start()
    for load in loads:
        load.start()

    e = ids_ref[...]
    s = slots_ref[...]
    gate = gates_ref[...].astype(F32)
    grp = e // L
    gi = iota((NG, TOK), 0)
    o0 = (grp[0:1] == gi).astype(F32)
    o1 = (grp[1:2] == gi).astype(F32)
    tri = (iota((TOK, TOK), 0) < iota((TOK, TOK), 1)).astype(F32).astype(BF)
    c0 = jnp.dot(o0.astype(BF), tri, preferred_element_type=F32)
    c1 = jnp.dot(o1.astype(BF), tri, preferred_element_type=F32)
    total0 = jnp.sum(o0, axis=1, keepdims=True)
    rank0 = jnp.sum(o0 * c0, axis=0, keepdims=True)
    rank1 = jnp.sum(o1 * (c1 + total0), axis=0, keepdims=True)
    pos0 = (grp[0:1] * RG).astype(F32) + rank0
    pos1 = (grp[1:2] * RG).astype(F32) + rank1
    pi = iota((NP, TOK), 0).astype(F32)
    b0 = (pi == pos0).astype(F32)
    b1 = (pi == pos1).astype(F32)
    gx[...] = (b0 + b1).astype(BF)
    gs[...] = (b0 * gate[0:1] + b1 * gate[1:2]).astype(BF)
    bk[0] = b0.astype(BF)
    bk[1] = b1.astype(BF)

    v = (e - grp * L) * XC + x * CAP + s
    v0 = jnp.broadcast_to(v[0:1], (8, TOK)).astype(F32).astype(BF)
    v1 = jnp.broadcast_to(v[1:2], (8, TOK)).astype(F32).astype(BF)
    val = lax.dot_general(v0, bk[0], NT, preferred_element_type=F32) + lax.dot_general(
        v1, bk[1], NT, preferred_element_type=F32
    )
    own = (iota((NG, NP), 1) // RG == iota((NG, NP), 0)).astype(F32)
    pp = iota((NP, LANES), 0)
    pick = (iota((NP, LANES), 1) == x * RG + lax.rem(pp, RG)).astype(F32).astype(BF)
    meta = jnp.dot((own * val[0:1]).astype(BF), pick, preferred_element_type=F32)
    for g in range(NG):
        ms[g] = jnp.broadcast_to(meta[g : g + 1], (8, LANES))

    def row_copy(k, dx):
        g = node_of(y - offset[k], x + dx)
        return pltpu.make_async_remote_copy(
            s1.at[g], r1.at[k, x], n_send.at[k, dx], n_recv.at[k, dx],
            device_id=(g, l), device_id_type=MESH,
        )

    def meta_copy(k, dx):
        g = node_of(y - offset[k], x + dx)
        return pltpu.make_async_remote_copy(
            ms.at[g], mr.at[k, x], m_send.at[k, dx], m_recv.at[k, dx],
            device_id=(g, l), device_id_type=MESH,
        )

    def row_arrival(k, dx):
        xs = lax.rem(x - dx + X, X)
        return pltpu.make_async_remote_copy(
            s1.at[n], r1.at[k, xs], n_send.at[k, dx], n_recv.at[k, dx],
            device_id=(node_of(y + offset[k], xs), l), device_id_type=MESH,
        )

    def meta_arrival(k, dx):
        xs = lax.rem(x - dx + X, X)
        return pltpu.make_async_remote_copy(
            ms.at[n], mr.at[k, xs], m_send.at[k, dx], m_recv.at[k, dx],
            device_id=(node_of(y + offset[k], xs), l), device_id_type=MESH,
        )

    def z_copy(k, d):
        j = lax.rem(l + d, L)
        return pltpu.make_async_remote_copy(
            s2.at[k, j], r2.at[k, l, :, pl.ds(BW, AW)], z_send.at[k, d], z_recv.at[k, d],
            device_id=(n, j), device_id_type=MESH,
        )

    def z_arrival(k, d):
        j = lax.rem(l - d + L, L)
        return pltpu.make_async_remote_copy(
            s2.at[k, j], r2.at[k, j, :, pl.ds(BW, AW)], z_send.at[k, d], z_recv.at[k, d],
            device_id=(n, j), device_id_type=MESH,
        )

    def b_copy(k, d):
        j = lax.rem(l + d, L)
        return pltpu.make_async_remote_copy(
            s3.at[k, j], r3.at[k, l], b_send.at[k, d], b_recv.at[k, d],
            device_id=(n, j), device_id_type=MESH,
        )

    def b_arrival(k, d):
        j = lax.rem(l - d + L, L)
        return pltpu.make_async_remote_copy(
            s3.at[k, j], r3.at[k, j], b_send.at[k, d], b_recv.at[k, d],
            device_id=(n, j), device_id_type=MESH,
        )

    def home_copy(k, dx):
        xs = lax.rem(x + dx, X)
        return pltpu.make_async_remote_copy(
            s4.at[k, xs], r4.at[n], h_send.at[k, dx], h_recv.at[k, dx],
            device_id=(node_of(y + offset[k], xs), l), device_id_type=MESH,
        )

    def home_arrival(k, dx):
        g = node_of(y - offset[k], x - dx)
        return pltpu.make_async_remote_copy(
            s4.at[k, x], r4.at[g], h_send.at[k, dx], h_recv.at[k, dx],
            device_id=(g, l), device_id_type=MESH,
        )

    def tiles(width, tile, body):
        def step(i, carry):
            body(pl.multiple_of(i * tile, tile))
            return carry

        lax.fori_loop(0, width // tile, step, 0)

    sent = []

    def send(copy):
        copy.start()
        sent.append(copy)

    td = min(512, BW)
    th = min(256, H)

    def t_copy(dz):
        j = lax.rem(zz + dz, Z) * 2 + core
        return pltpu.make_async_remote_copy(
            tb.at[l], tb.at[l], t_send.at[dz], t_recv.at[dz],
            device_id=(n, j), device_id_type=MESH,
        )

    def t_arrival(dz):
        j = lax.rem(zz - dz + Z, Z) * 2 + core
        return pltpu.make_async_remote_copy(
            tb.at[j], tb.at[j], t_send.at[dz], t_recv.at[dz],
            device_id=(n, j), device_id_type=MESH,
        )

    def f_copy(dz):
        j = lax.rem(zz - dz + Z, Z) * 2 + core
        return pltpu.make_async_remote_copy(
            tb.at[j], tb.at[j], f_send.at[dz], f_recv.at[dz],
            device_id=(n, l + 1 - 2 * core), device_id_type=MESH,
        )

    def f_arrival(dz):
        j = lax.rem(zz - dz + Z, Z) * 2 + 1 - core
        return pltpu.make_async_remote_copy(
            tb.at[j], tb.at[j], f_send.at[dz], f_recv.at[dz],
            device_id=(n, l + 1 - 2 * core), device_id_type=MESH,
        )

    def id_copy(d):
        j = lax.rem(l + d, L)
        return pltpu.make_async_remote_copy(
            ms2, mb.at[l], i_send.at[d], i_recv.at[d],
            device_id=(n, j), device_id_type=MESH,
        )

    def id_arrival(d):
        j = lax.rem(l - d + L, L)
        return pltpu.make_async_remote_copy(
            ms2, mb.at[j], i_send.at[d], i_recv.at[d],
            device_id=(n, j), device_id_type=MESH,
        )

    def g_copy(k, dx):
        g = node_of(y - offset[k], x + dx)
        return pltpu.make_async_remote_copy(
            sb.at[g], rb.at[n], g_send.at[k, dx], g_recv.at[k, dx],
            device_id=(g, l), device_id_type=MESH,
        )

    def g_arrival(k, dx):
        g = node_of(y + offset[k], x - dx)
        return pltpu.make_async_remote_copy(
            sb.at[n], rb.at[g], g_send.at[k, dx], g_recv.at[k, dx],
            device_id=(g, l), device_id_type=MESH,
        )

    def token_send(_):
        for load in rows_in:
            load.wait()
        tb[l] = tok_ref[:, 0:BW]
        ms2[...] = jnp.concatenate([e, s, e, s], axis=0).astype(F32)
        mb[l] = ms2[...]
        pl.semaphore_wait(barrier, NG + L - 2)
        for d in range(1, L):
            send(id_copy(d))
        for dz in range(1, Z):
            send(t_copy(dz))
        send(f_copy(0))

    def token_forward(_):
        for dz in range(1, Z):
            t_arrival(dz).wait_recv()
            send(f_copy(dz))

    def token_route(_):
        for d in range(1, L):
            id_arrival(d).wait_recv()
        row = iota((NG * LC, TOK), 0).astype(F32)
        for j in range(L):
            m = mb[j].astype(jnp.int32)
            ej, sj = m[0:2], m[2:4]
            gj = ej // L
            place = jnp.where(ej - gj * L == l, gj * LC + j * CAP + sj, -1).astype(F32)
            hit = (row == place[0:1]) | (row == place[1:2])
            oh[:, j * TOK : (j + 1) * TOK] = hit.astype(F32).astype(BF)
        for dz in range(Z):
            f_arrival(dz).wait_recv()

        def body(c):
            rows = tb[:, :, pl.ds(c, th)].reshape(L * TOK, th)
            a = jnp.dot(oh[...], rows, preferred_element_type=F32)
            sb[:, :, pl.ds(c, th)] = a.astype(BF).reshape(NG, LC, th)

        tiles(BW, th, body)
        for k in range(Y):
            for dx in range(X):
                if k or dx:
                    send(g_copy(k, dx))
        rb[n] = sb[n]

    def token_take(k):
        for dx in range(X):
            if k or dx:
                g_arrival(k, dx).wait_recv()
        out, col = iota((ROWS, ROWS), 0), iota((ROWS, ROWS), 1)
        src = lax.rem(out, XC) // CAP * LC + out // XC * CAP + lax.rem(out, CAP)
        perm = (src == col).astype(F32).astype(BF)
        nodes = pl.ds(lax.rem(y + offset[k], Y) * X, X)

        def body(c):
            rows = rb[nodes, :, pl.ds(c, td)].reshape(ROWS, td)
            a = jnp.dot(perm, rows, preferred_element_type=F32)
            r2[k, :, :, pl.ds(c, td)] = a.astype(BF).reshape(L, XC, td)

        tiles(BW, td, body)

    def node_send(k):
        yy = lax.rem(y - offset[k] + Y, Y)
        rows = pl.ds(pl.multiple_of(yy * XR, XR), XR)
        groups = pl.ds(yy * X, X)

        def own_x(c):
            a = jnp.dot(gx[rows, :], tok_ref[:, pl.ds(c + BW, td)], preferred_element_type=F32)
            s1[groups, :, pl.ds(c, td)] = a.astype(BF).reshape(X, RG, td)

        def own_scaled(c):
            b = jnp.dot(gs[rows, :], cot_ref[:, pl.ds(c, td)], preferred_element_type=F32)
            s1[groups, :, pl.ds(c + D - BW, td)] = b.astype(BF).reshape(X, RG, td)

        tiles(D - BW, td, own_x)
        tiles(D, td, own_scaled)
        for dx in range(X):
            if k or dx:
                send(meta_copy(k, dx))
                send(row_copy(k, dx))
            else:
                r1[0, x] = s1[n]
                mr[0, x] = ms[n]

    def z_step(k):
        for dx in range(X):
            if k or dx:
                meta_arrival(k, dx).wait_recv()
                row_arrival(k, dx).wait_recv()
        target = mr[k, 0]
        for xs in range(1, X):
            target = target + mr[k, xs]
        place = iota((ROWS, XR), 0).astype(F32) == target[0:1, :XR]
        pk[k] = place.astype(F32)
        perm = place.astype(F32).astype(BF)

        def body(c):
            rows = r1[k, :, :, pl.ds(c, td)].reshape(XR, td)
            a = jnp.dot(perm, rows, preferred_element_type=F32)
            s2[k, :, :, pl.ds(c, td)] = a.astype(BF).reshape(L, XC, td)

        tiles(AW, td, body)
        for d in range(1, L):
            send(z_copy(k, d))
        r2[k, l, :, BW:] = s2[k, l]

    saves = []

    arrived = set()

    def z_wait(k):
        if k not in arrived:
            arrived.add(k)
            for d in range(1, L):
                z_arrival(k, d).wait_recv()

    def compute(k):
        token_take(k)
        z_wait(k)
        if k == 0:
            for load in loads:
                load.wait()

        def fwd(i, u):
            c = pl.multiple_of(i * th, th)
            xr = r2[k, :, :, 0:D].reshape(ROWS, D)
            sr = r2[k, :, :, D : 2 * D].reshape(ROWS, D)
            gp = jnp.dot(xr, wg[:, pl.ds(c, th)], preferred_element_type=F32)
            up = jnp.dot(xr, wu[:, pl.ds(c, th)], preferred_element_type=F32)
            dh = lax.dot_general(sr, wd[pl.ds(c, th), :], NT, preferred_element_type=F32)
            sig = jax.nn.sigmoid(gp)
            act = gp * sig
            hf = act * up
            ht[pl.ds(c, th), k * ROWS : (k + 1) * ROWS] = hf.T.astype(BF)
            dg[k, :, pl.ds(c, th)] = (dh * up * sig * (1.0 + gp * (1.0 - sig))).astype(BF)
            du[k, :, pl.ds(c, th)] = (dh * act).astype(BF)
            return u + jnp.sum(hf * dh, axis=1, keepdims=True)

        u = lax.fori_loop(0, H // th, fwd, jnp.zeros((ROWS, 1), F32))

        def bwd(c):
            a = lax.dot_general(dg[k], wg[pl.ds(c, th), :], NT, preferred_element_type=F32)
            a = a + lax.dot_general(du[k], wu[pl.ds(c, th), :], NT, preferred_element_type=F32)
            s3[k, :, :, pl.ds(c, th)] = a.astype(BF).reshape(L, XC, th)

        tiles(D, th, bwd)
        hi = u.astype(BF).astype(F32)
        col = iota((ROWS, LANES), 1)
        both = jnp.where(col == 0, hi, jnp.where(col == 1, u - hi, 0.0))
        s3[k, :, :, D:DR] = both.astype(BF).reshape(L, XC, LANES)
        for i, (src, dst) in enumerate(((dg, dg_hbm), (du, du_hbm))):
            save = pltpu.make_async_copy(src.at[k], dst.at[k], out_sem.at[k, i])
            save.start()
            saves.append(save)

    def keep(k):
        def body(c):
            rows = r2[k, :, :, pl.ds(c, th)].reshape(ROWS, th)
            xt[pl.ds(c, th), k * ROWS : (k + 1) * ROWS] = rows.astype(F32).T.astype(BF)

        tiles(D, th, body)
        lanes = pl.ds(k * ROWS, ROWS)
        for i, (src, dst) in enumerate(
            (
                (r2.at[k, :, :, pl.ds(D, D)], sc_hbm.at[k]),
                (xt.at[:, lanes], xt_hbm.at[:, lanes]),
                (ht.at[:, lanes], ht_hbm.at[:, lanes]),
            )
        ):
            save = pltpu.make_async_copy(src, dst, out_sem.at[k, 2 + i])
            save.start()
            saves.append(save)

    def back_send(k):
        for d in range(1, L):
            send(b_copy(k, d))
        r3[k, l] = s3[k, l]

    def home_step(k):
        for d in range(1, L):
            b_arrival(k, d).wait_recv()
        perm = pk[k].T.astype(BF)

        def body(c):
            rows = r3[k, :, :, pl.ds(c, td)].reshape(ROWS, td)
            a = jnp.dot(perm, rows, preferred_element_type=F32)
            s4[k, :, :, pl.ds(c, td)] = a.astype(BF).reshape(X, RG, td)

        tiles(D, td, body)
        a = jnp.dot(perm, r3[k, :, :, D:DR].reshape(ROWS, LANES), preferred_element_type=F32)
        s4[k, :, :, D:DR] = a.astype(BF).reshape(X, RG, LANES)
        for dx in range(X):
            if k or dx:
                send(home_copy(k, dx))
            else:
                own_home.start()

    own_home = pltpu.make_async_copy(s4.at[0, x], r4.at[n], w_sem.at[5])
    phases = dict(t=token_send, f=token_forward, g=token_route, n=node_send, z=z_step, w=z_wait, c=compute, b=back_send, k=keep, h=home_step)
    for phase in PLAN:
        phases[phase[0]](int(phase[1]))

    for k in range(Y):
        for dx in range(X):
            if k or dx:
                home_arrival(k, dx).wait_recv()
    own_home.wait()
    for save in saves:
        save.wait()
    for copy in sent:
        copy.wait_send()


def outputs_kernel(
    tile,
    xt_hbm, sc_hbm, ht_hbm, dg_hbm, du_hbm, home_hbm, bk_ref, gate_ref,
    og_hbm, ou_hbm, od_hbm, gin_hbm, ggate_ref,
    xt, sc, ht, dg, du, home, og, ou, od, gin, in_sem, out_sem,
):
    D, H = xt.shape[0], ht.shape[0]
    parts = 4
    depth = D // parts
    pending = []

    def load(i, src, dst):
        copy = pltpu.make_async_copy(src, dst, in_sem.at[i])
        copy.start()
        return copy

    dg_load = load(0, dg_hbm, dg)
    xt_loads = [
        load(1 + i, xt_hbm.at[pl.ds(i * depth, depth)], xt.at[pl.ds(i * depth, depth)])
        for i in range(parts)
    ]
    du_load = load(parts + 1, du_hbm, du)
    ht_load = load(parts + 2, ht_hbm, ht)
    sc_load = load(parts + 3, sc_hbm, sc)
    home_load = load(parts + 4, home_hbm, home)

    def save(src, dst):
        copy = pltpu.make_async_copy(src, dst, out_sem.at[len(pending)])
        copy.start()
        pending.append(copy)

    def product(left, right, out, dst, waits):
        height = left.shape[0]
        for i, r in enumerate(range(0, height, tile)):
            if r in waits:
                waits[r].wait()
            rows = pl.ds(r, tile)
            right_rows = right[...].reshape(-1, right.shape[-1])
            a = jnp.dot(left[rows, :], right_rows, preferred_element_type=F32)
            out[rows, :] = a.astype(BF)
            save(out.at[rows], dst.at[0, rows])

    dg_load.wait()
    product(xt, dg, og, og_hbm, {i * depth: copy for i, copy in enumerate(xt_loads)})
    du_load.wait()
    product(xt, du, ou, ou_hbm, {})
    ht_load.wait()
    sc_load.wait()
    product(ht, sc, od, od_hbm, {})

    home_load.wait()
    both = (bk_ref[0].astype(F32) + bk_ref[1].astype(F32)).T.astype(BF)
    back = home[...].reshape(-1, home.shape[-1])
    gin[...] = jnp.dot(both, back[:, :D], preferred_element_type=F32).astype(BF)
    save(gin, gin_hbm)
    gate = gate_ref[...].astype(F32)
    sums = back[:, D:].astype(F32).T.astype(BF)
    for k in range(2):
        t = jnp.dot(sums, bk_ref[k], preferred_element_type=F32)
        ggate_ref[k : k + 1, :] = ((t[0:1] + t[1:2]) / gate[k : k + 1]).astype(BF)
    for copy in pending:
        copy.wait()


def local(grid_y, tokens, cotangent, gates, expert_ids, slots, w_gate, w_up, w_down):
    tok, width = tokens.shape
    hidden = w_gate.shape[2]
    n_node = lax.axis_size("node")
    n_local = lax.axis_size("local")
    Y, X, L = grid_y, n_node // grid_y, n_local
    cap = 4 * tok // (n_node * n_local)
    RG = 2 * tok // n_node
    D, H = width, hidden
    XC, XR, ROWS, NP, DR = X * cap, X * RG, L * X * cap, 2 * tok, width + LANES
    vmem = pl.BlockSpec(memory_space=pltpu.VMEM)
    hbm = pl.BlockSpec(memory_space=pl.ANY)
    sem = pltpu.SemaphoreType.DMA
    shape = jax.ShapeDtypeStruct
    macs = 5 * Y * ROWS * D * H
    home, bk, sc, xt, ht, dg, du = pl.pallas_call(
        functools.partial(layer_kernel, (Y, X, L, RG, cap, D, H)),
        out_shape=(
            shape((n_node, RG, DR), BF),
            shape((2, NP, tok), BF),
            shape((Y, L, XC, D), BF),
            shape((D, Y * ROWS), BF),
            shape((H, Y * ROWS), BF),
            shape((Y, ROWS, H), BF),
            shape((Y, ROWS, H), BF),
        ),
        in_specs=[vmem] * 3 + [hbm] * 5,
        out_specs=(hbm, vmem, hbm, hbm, hbm, hbm, hbm),
        scratch_shapes=[
            pltpu.VMEM((tok, D), BF),
            pltpu.VMEM((tok, D), BF),
            pltpu.VMEM((D, H), BF),
            pltpu.VMEM((D, H), BF),
            pltpu.VMEM((H, D), BF),
            pltpu.VMEM((NP, tok), BF),
            pltpu.VMEM((NP, tok), BF),
            pltpu.VMEM((n_node, 8, LANES), F32),
            pltpu.VMEM((Y, X, 8, LANES), F32),
            pltpu.VMEM((n_node, RG, 3 * D // 2), BF),
            pltpu.VMEM((Y, X, RG, 3 * D // 2), BF),
            pltpu.VMEM((Y, ROWS, XR), F32),
            pltpu.VMEM((Y, L, XC, 3 * D // 2), BF),
            pltpu.VMEM((Y, L, XC, 2 * D), BF),
            pltpu.VMEM((D, Y * ROWS), BF),
            pltpu.VMEM((H, Y * ROWS), BF),
            pltpu.VMEM((Y, ROWS, H), BF),
            pltpu.VMEM((Y, ROWS, H), BF),
            pltpu.VMEM((Y, L, XC, DR), BF),
            pltpu.VMEM((Y, L, XC, DR), BF),
            pltpu.VMEM((Y, X, RG, DR), BF),
            pltpu.VMEM((L, tok, D // 2), BF),
            pltpu.VMEM((8, tok), F32),
            pltpu.VMEM((L, 8, tok), F32),
            pltpu.VMEM((n_node * L * cap, L * tok), BF),
            pltpu.VMEM((n_node, L * cap, D // 2), BF),
            pltpu.VMEM((n_node, L * cap, D // 2), BF),
            sem((6,)),
            sem((Y, 5)),
            sem((Y, X)),
            sem((Y, X)),
            sem((Y, X)),
            sem((Y, X)),
            sem((Y, L)),
            sem((Y, L)),
            sem((Y, L)),
            sem((Y, L)),
            sem((Y, X)),
            sem((Y, X)),
            sem((L // 2,)),
            sem((L // 2,)),
            sem((L // 2,)),
            sem((L // 2,)),
            sem((L,)),
            sem((L,)),
            sem((Y, X)),
            sem((Y, X)),
        ],
        compiler_params=pltpu.CompilerParams(
            collective_id=0, has_side_effects=True, vmem_limit_bytes=54 * 2**20
        ),
        cost_estimate=pl.CostEstimate(
            flops=2 * macs, bytes_accessed=24 * 2**20, transcendentals=Y * ROWS * H
        ),
        name="routed_layer",
    )(expert_ids.T, slots.T, gates.T, tokens, cotangent, w_gate, w_up, w_down)
    sc = sc.reshape(Y, ROWS, D)
    tile = min(256, H)
    gg, gu, gd, gin, ggate = pl.pallas_call(
        functools.partial(outputs_kernel, tile),
        out_shape=(
            shape((1, D, H), BF),
            shape((1, D, H), BF),
            shape((1, H, D), BF),
            shape((tok, D), BF),
            shape((2, tok), BF),
        ),
        in_specs=[hbm] * 6 + [vmem] * 2,
        out_specs=(hbm, hbm, hbm, hbm, vmem),
        scratch_shapes=[
            pltpu.VMEM((D, Y * ROWS), BF),
            pltpu.VMEM((Y, ROWS, D), BF),
            pltpu.VMEM((H, Y * ROWS), BF),
            pltpu.VMEM((Y, ROWS, H), BF),
            pltpu.VMEM((Y, ROWS, H), BF),
            pltpu.VMEM((n_node, RG, DR), BF),
            pltpu.VMEM((D, H), BF),
            pltpu.VMEM((D, H), BF),
            pltpu.VMEM((H, D), BF),
            pltpu.VMEM((tok, D), BF),
            sem((9,)),
            sem(((2 * D + H) // tile + 1,)),
        ],
        compiler_params=pltpu.CompilerParams(vmem_limit_bytes=60 * 2**20),
        cost_estimate=pl.CostEstimate(
            flops=6 * Y * ROWS * D * H, bytes_accessed=20 * 2**20, transcendentals=0
        ),
        name="weight_grads",
    )(xt, sc, ht, dg, du, home, bk, gates.T)
    return gin, ggate.T, gg, gu, gd


def solution(mesh):
    both = ("node", "local")
    n_node = mesh.shape["node"]
    grid_y = 1
    while (2 * grid_y) ** 2 <= n_node and n_node % (2 * grid_y) == 0:
        grid_y *= 2
    placed = (P(both, None),) * 5 + (P(both, None, None),) * 3
    return jax.shard_map(
        functools.partial(local, grid_y),
        mesh=mesh,
        in_specs=placed,
        out_specs=(P(both, None),) * 2 + (P(both, None, None),) * 3,
        check_vma=False,
    )
```

time: 127 us -> 106 us (0.83)
  Pallas kernels: 120 us -> 105 us
  local copies, waits for them, and re-layouts: 4.98 us -> 0 us
    pallas_call x1, Pallas kernels: 109 us -> 93.6 us  [local(): pl.pallas_call(functools.partial(layer_kernel, (Y, X, L, RG, cap, D, H)),...]
    unnamed x12 -> x0, local copies, waits for them, and re-layouts: 4.98 us -> none
where the time goes in v2:
time: 106 us
  Pallas kernels  105 us (99%)
    pallas_call x1, Pallas kernels, local(): pl.pallas_call(functools.partial(layer_kernel, (Y, X, L, RG, cap, D, H)),...  93.6 us
    pallas_call x1, Pallas kernels, local(): pl.pallas_call(functools.partial(outputs_kernel, tile), out_shape=(shape(...  11.8 us

profile of v2, /device:TPU:1, one launch (start us, length us, event | category | flops | bytes accessed | tf_op | source)
XLA Modules:
  0.0 106.2 jit_solution(15745497624663019962)
XLA Ops:
  0.6 93.6 %routed_layer.1 = (bf16[16,16,2176]{2,1,0:T(8,128)(2,1)}, bf16[2,256,128]{2,1,0:T(8,128)(2,1)}, bf16[4,8,16,2048]{3,2,1,0:T(8,128)(2,1)}, bf16[2048,512]{1,0:T(8...) custom-call(s32[2,128]{1,0:T(2,128)} %bitcast.5, ...), custom_call_target="tpu_custom_call" | custom-call | flops 10737418240 | bytes 25165824 | tf_op jit(solution)/shard_map/routed_layer/pallas_call | solution.py:550
  94.3 11.8 %weight_grads.1 = (bf16[1,2048,1024]{2,1,0:T(8,128)(2,1)}, bf16[1,2048,1024]{2,1,0:T(8,128)(2,1)}, bf16[1,1024,2048]{2,1,0:T(8,128)(2,1)}, bf16[128,2048]{1,0:T(8,128)(2,1)}, bf16[2,128]{1,0:T(2,128)(2,1)}) custom-call(bf16[2048,512]{1,0:T(8,128)(2,1)} %get-tuple-element.17.xt_hbm, bf16[4,128,2048]{2,1,0:T(8,128)(2,1)} %bitcast.9, ...), custom_call_target="tpu_custom_call" | custom-call | flops 6442450944 | bytes 20971520 | tf_op jit(solution)/shard_map/weight_grads/pallas_call | solution.py:622

commit v3 on v2

--- a/solution.py
+++ b/solution.py
@@ -12,8 +12,8 @@
 F32 = jnp.float32
 LANES = 128
 PLAN = (
-    "t0", "n0", "n1", "n2", "n3", "z0", "f0", "z1", "g0", "z2", "c0", "z3", "b0", "k0", "c1",
-    "b1", "k1", "c2", "k2", "w3", "b2", "c3", "b3", "k3", "h0", "h1", "h2", "h3",
+    "t0", "n0", "n1", "n2", "n3", "z0", "f0", "z1", "g0", "z2", "c0", "z3", "b0", "c1", "b1",
+    "k0", "c2", "k1", "w3", "b2", "c3", "b3", "h0", "k2", "h1", "k3", "h2", "h3",
 )
 NT = (((1,), (1,)), ((), ()))
 TN = (((0,), (0,)), ((), ()))

time: 106 us -> 106 us (level)
  no operation moved by 1% of the time
where the time goes in v3:
time: 106 us
  Pallas kernels  105 us (99%)
    pallas_call x1, Pallas kernels, local(): pl.pallas_call(functools.partial(layer_kernel, (Y, X, L, RG, cap, D, H)),...  93.7 us
    pallas_call x1, Pallas kernels, local(): pl.pallas_call(functools.partial(outputs_kernel, tile), out_shape=(shape(...  11.8 us

profile of v3, /device:TPU:1, one launch (start us, length us, event | category | flops | bytes accessed | tf_op | source)
XLA Modules:
  0.0 106.2 jit_solution(10916587292225859481)
XLA Ops:
  0.6 93.7 %routed_layer.1 = (bf16[16,16,2176]{2,1,0:T(8,128)(2,1)}, bf16[2,256,128]{2,1,0:T(8,128)(2,1)}, bf16[4,8,16,2048]{3,2,1,0:T(8,128)(2,1)}, bf16[2048,512]{1,0:T(8...) custom-call(s32[2,128]{1,0:T(2,128)} %bitcast.5, ...), custom_call_target="tpu_custom_call" | custom-call | flops 10737418240 | bytes 25165824 | tf_op jit(solution)/shard_map/routed_layer/pallas_call | solution.py:550
  94.3 11.8 %weight_grads.1 = (bf16[1,2048,1024]{2,1,0:T(8,128)(2,1)}, bf16[1,2048,1024]{2,1,0:T(8,128)(2,1)}, bf16[1,1024,2048]{2,1,0:T(8,128)(2,1)}, bf16[128,2048]{1,0:T(8,128)(2,1)}, bf16[2,128]{1,0:T(2,128)(2,1)}) custom-call(bf16[2048,512]{1,0:T(8,128)(2,1)} %get-tuple-element.17.xt_hbm, bf16[4,128,2048]{2,1,0:T(8,128)(2,1)} %bitcast.9, ...), custom_call_target="tpu_custom_call" | custom-call | flops 6442450944 | bytes 20971520 | tf_op jit(solution)/shard_map/weight_grads/pallas_call | solution.py:622
